TPU v7x, 32 devices: a whole 2x2x4 slice. The times are simulated.
32 devices in a mesh: grow: 4 (over y, x), gcol: 8 (over z, core).
Axes of the slice: x: 2, y: 2, z: 4, core: 2. Of those that a mesh axis runs over, the one named last changes fastest.
Arguments:
- screened: bfloat16 [2, 16384, 16384], P(None, 'grow', 'gcol'), may hold values from -6 to 6
- elements: bfloat16 [2, 1024, 16384], P(None, None, ('grow', 'gcol')), may hold values from -0.046875 to 0.046875
- energy_grid: float32 [256], replicated, may hold values from -3 to 3
- band_index: int32 [256], replicated, may hold values from 0 to 255
- energy_index: int32 [4, 16], replicated, may hold values from 0 to 255
Outputs:
- sigma: float32 [2, 4, 16], replicated
All inputs are finite; a program needn't handle non-finite values.
Results may differ from a plain program's by a relative error of at most 0.0003.
Values may be sent and summed in bfloat16 or wider, within the bound.
A program may use at most 192 MiB of HBM per device.

v0:
```python
import jax
import jax.numpy as jnp
from jax import lax
from jax.sharding import PartitionSpec as P


def spread(block, axis, source):
    block = jnp.where(lax.axis_index(axis) == source, block, jnp.zeros_like(block))
    return lax.psum(block, axis)


def weights(energy_grid, band_index, energy_index):
    points = lax.broadcasted_iota(jnp.int32, (1, energy_grid.shape[0]), 1)
    band_energy = jnp.sum(
        jnp.where(band_index[:, None] == points, energy_grid[None, :], 0.0), axis=-1
    )
    eval_energy = jnp.sum(
        jnp.where(energy_index[:, :, None] == points[None], energy_grid[None, None, :], 0.0),
        axis=-1,
    )
    offset = eval_energy[:, None, :] - band_energy[None, :, None]
    denom = offset * offset + 0.25
    return (offset / denom, -0.5 / denom)


def weigh(s_re, s_im, wre, wim):
    outer = wre.shape[0]
    summed = wre.shape[1]
    sre = s_re.reshape(outer, summed)[:, :, None]
    sim = s_im.reshape(outer, summed)[:, :, None]
    scale = summed ** (-0.5)
    out_re = scale * jnp.sum(wre * sre - wim * sim, axis=1)
    out_im = scale * jnp.sum(wre * sim + wim * sre, axis=1)
    return (out_re, out_im)


def local(screened, elements, energy_grid, band_index, energy_index):
    row_part = lax.all_gather(elements, "gcol", axis=2, tiled=True)
    ncol = screened.shape[2]
    place = lax.axis_index("gcol")
    half = lax.dynamic_slice_in_dim(row_part, place % 2 * ncol, ncol, 2)
    col_part = spread(half, "grow", place // 2)
    prod = jnp.einsum("mph,wgh->mpwg", col_part, screened, preferred_element_type=jnp.float32)
    yre = prod[0, :, 0] - prod[1, :, 1]
    yim = prod[1, :, 0] + prod[0, :, 1]
    rre = row_part[0].astype(jnp.float32)
    rim = row_part[1].astype(jnp.float32)
    s_re = jnp.sum(rre * yre + rim * yim, axis=-1)
    s_im = jnp.sum(rre * yim - rim * yre, axis=-1)
    wre, wim = weights(energy_grid, band_index, energy_index)
    total_re, total_im = lax.psum((s_re, s_im), ("grow", "gcol"))
    out_re, out_im = weigh(total_re, total_im, wre, wim)
    return jnp.stack([out_re, out_im])


def solution(mesh):
    in_specs = (P(None, "grow", "gcol"), P(None, None, ("grow", "gcol")), P(), P(), P())
    out_specs = P()
    return jax.shard_map(local, mesh=mesh, in_specs=in_specs, out_specs=out_specs, check_vma=False)
```

profile of v0, /device:TPU:0, one launch (start us, length us, event | category | flops | bytes accessed | tf_op | source)
XLA Modules:
  0.0 498.3 jit_solution(16321079630531870284)
XLA Ops:
  6.5 0.0 copy-start.1
  6.5 0.0 copy-start.3
  6.5 0.0 copy-start.4
  6.5 0.0 all-gather.2.cloned.1.call-start
  6.5 0.7 all-gather.2.cloned.1.call-update
  7.3 0.0 all-reduce.3.cloned.1.call-start
  7.3 155.5 %all-gather.2.cloned.1.call-done = bf16[2,1024,4096]{2,1,0:T(8,128)(2,1)} async-done(((bf16[2,1024,512]{2,1,0:T(8,128)(2,1)}), bf16[2,1024,4096]{2,1,0:T(8,128)(2,1)}) %all-gather.2.cloned.1.call-update) | async-done | bytes 16777232 | tf_op jit(solution)/shard_map/all_gather | solution.py:38
  162.8 9.7 %dynamic-slice_select_fusion = bf16[2,1024,2048]{2,1,0:T(8,128)(2,1)} fusion(bf16[2,1024,4096]{2,1,0:T(8,128)(2,1)} %all-gather.2.cloned.1.call-done, s32[]{:T(128)S(6)} %select_n.35, pred[]{:T(512)S(6)} %eq.37), kind=kLoop, calls=%fused_computation.17 | loop fusion | flops 4194304 | bytes 16777220 | tf_op jit(solution)/shard_map/jit(_where)/select_n | solution.py:8
  172.5 0.0 all-reduce.3.cloned.1.call-update
  172.5 0.0 copy-done.1
  172.5 0.0 copy-done.3
  172.5 0.7 select_reduce_fusion.1
  173.3 0.0 copy-done.4
  173.3 0.8 select_reduce_fusion
  174.0 168.9 %all-reduce.3.cloned.1.call-done = bf16[2,1024,2048]{2,1,0:T(8,128)(2,1)} async-done(((bf16[2,1024,2048]{2,1,0:T(8,128)(2,1)}), bf16[2,1024,2048]{2,1,0:T(8,128)(2,1)}) %all-reduce.3.cloned.1.call-update) | async-done | bytes 8388624 | tf_op jit(solution)/shard_map/psum | solution.py:9
  342.9 79.4 %fusion = f32[2,1024,2,4096]{3,1,2,0:T(8,128)} fusion(bf16[2,4096,2048]{2,1,0:T(8,128)(2,1)} %param.5, bf16[2,1024,2048]{2,1,0:T(8,128)(2,1)} %all-reduce.3.cloned.1.call-done), kind=kOutput, calls=%fused_computation | convolution fusion | flops 68719476736 | bytes 109051904 | tf_op jit(solution)/shard_map/mph,wgh->mpwg/dot_general | solution.py:43
  422.4 0.0 copy-start
  422.4 0.0 copy-start.2
  422.4 28.2 %fusion.3 = (f32[1024]{0:T(1024)S(1)}, f32[1024]{0:T(1024)S(1)}) fusion(bf16[2,1024,4096]{2,1,0:T(8,128)(2,1)} %all-gather.2.cloned.1.call-done, f32[2,1024,2,4096]{3,1,2,0:T(8,128)} %fusion), kind=kLoop, calls=%fused_computation.7 | loop fusion | flops 50329600 | bytes 83894272 | tf_op jit(solution)/shard_map/reduce_sum | solution.py:48
  450.6 40.1 %all-reduce = (f32[4,256]{1,0:T(4,128)S(1)}, f32[4,256]{1,0:T(4,128)S(1)}) all-reduce(f32[4,256]{1,0:T(4,128)S(1)} %mul.85, f32[4,256]{1,0:T(4,128)S(1)} %mul.80), channel_id=1, replica_groups=mesh['grow'=4,'gcol'=8] {'grow','gcol'}, use_global_device_ids=true, to_apply=%region_6.7 | all-reduce | flops 2048 | bytes 16384 | tf_op jit(solution)/shard_map/psum | solution.py:51
  490.7 0.0 copy-done
  490.7 0.0 copy-done.2
  490.7 0.2 subtract_reduce_fusion
  490.9 0.6 pad_maximum_fusion
  (3 shorter events, 0.0 us)
Async XLA Ops:
  6.5 166.0 %copy-start.1 = (f32[256]{0:T(256)S(1)}, f32[256]{0:T(256)}, u32[]{:S(2)}) copy-start(f32[256]{0:T(256)} %param.7) | copy-start | bytes 3076
  6.5 166.0 %copy-start.3 = (s32[4,16]{1,0:T(4,128)S(1)}, s32[4,16]{1,0:T(4,128)}, u32[]{:S(2)}) copy-start(s32[4,16]{1,0:T(4,128)} %param.9) | copy-start | bytes 772
  6.5 166.7 %copy-start.4 = (s32[256]{0:T(256)S(1)}, s32[256]{0:T(256)}, u32[]{:S(2)}) copy-start(s32[256]{0:T(256)} %param.8) | copy-start | bytes 3076
  6.5 156.3 %all-gather.2.cloned.1.call-start = ((), (), s32[]{:S(2)}) async-start(), calls=%async_computation | async-start | bytes 18874368 | tf_op jit(solution)/shard_map/all_gather | solution.py:38
  7.3 335.7 %all-reduce.3.cloned.1.call-start = ((), (), s32[]{:S(2)}) async-start(), calls=%async_computation.1 | async-start | bytes 16777216 | tf_op jit(solution)/shard_map/psum | solution.py:9
  422.4 68.3 %copy-start = (f32[4,16]{1,0:T(4,128)S(1)}, f32[4,16]{1,0:T(4,128)}, u32[]{:S(2)}) copy-start(f32[4,16]{1,0:T(4,128)} %select_reduce_fusion.1) | copy-start | bytes 772
  422.4 68.3 %copy-start.2 = (f32[256]{0:T(256)S(1)}, f32[256]{0:T(256)}, u32[]{:S(2)}) copy-start(f32[256]{0:T(256)} %select_reduce_fusion) | copy-start | bytes 3076
Sparse Core Ops, SparseCore 0:
  9.0 153.7 all-gather.1
  172.6 170.2 all-reduce.2
where the time goes:
time: 499 us; the launch traced here: 498 us
  waiting for transfers between devices  325 us (65%)
  matrix products  79.4 us (16%)
  other arithmetic  40.1 us (8%)
  blocking collectives  40.1 us (8%)
  between operations  13.5 us (3%)
    psum x1, waiting for transfers between devices, spread(): return lax.psum(block, axis)  169 us
    all_gather x1, waiting for transfers between devices, local(): row_part = lax.all_gather(elements, 'gcol', axis=2, tiled=True)  155 us
    dot_general x1, matrix products, local(): jnp.einsum('mph,wgh->mpwg', col_part, screened, preferred_element_type=jn...  79.4 us
    psum x1, blocking collectives, local(): total_re, total_im = lax.psum((s_re, s_im), ('grow', 'gcol'))  40.1 us
    reduce_sum x1, other arithmetic, local(): s_re = jnp.sum(rre * yre + rim * yim, axis=-1)  28.2 us
  transfers between devices with their start and end apart: 2, of which 2 were waited for; matrix products, arithmetic and copies ran while one was open for 0% of the time, Pallas kernels for 0%

commit v1 on v0

v1 whole, which is shorter than its diff:
```python
import functools

import jax
import jax.numpy as jnp
from jax import lax
from jax.experimental import pallas as pl
from jax.experimental.pallas import tpu as pltpu
from jax.sharding import PartitionSpec as P

MESH = pl.DeviceIdType.MESH
CHUNKS = 4
TILE = 512


def kernel(
    ngrow, ngcol, w_ref, e_ref, grid_ref, band_ref, eidx_ref, out_ref,
    rows, cols, acc, wbuf, svec, tiles, mine,
    up_sem, dn_sem, pt_sem, lay_sem, row_sem, col_sem, loc_sem, own_sem, w_sem, t_send, t_recv,
):
    nq = ngcol // 2
    held = nq
    pairs = e_ref.shape[1]
    depth = e_ref.shape[2]
    width = w_ref.shape[2]
    chunk = pairs // CHUNKS
    r = lax.axis_index("grow")
    c = lax.axis_index("gcol")
    q = c // 2
    k = c % 2
    mate = 2 * q + 1 - k

    def swap(v):
        return v + (v // 2 % 2) * (1 - 2 * (v % 2))

    pos = swap(r)
    source = q
    after = swap(lax.rem(pos + 1, ngrow))
    before = swap(lax.rem(pos + ngrow - 1, ngrow))
    dist = lax.rem(pos - swap(source) + ngrow, ngrow)
    is_source = dist == 0

    near = jnp.minimum(q, nq - 1 - q)

    def order(t):
        alternate = jnp.where(t % 2 == 1, q - (t + 1) // 2, q + t // 2)
        rest = jnp.where(q > near, q - (t - near), q + (t - near))
        return jnp.where(t <= 2 * near, alternate, rest)

    barrier = pltpu.get_barrier_semaphore()
    for step in range(1, ngcol):
        pl.semaphore_signal(
            barrier, inc=1, device_id=(r, lax.rem(c + step, ngcol)), device_id_type=MESH
        )
    for step in range(1, ngrow):
        pl.semaphore_signal(
            barrier, inc=1, device_id=(lax.rem(r + step, ngrow), c), device_id_type=MESH
        )

    own = pltpu.make_async_copy(e_ref, rows.at[c], own_sem)
    own.start()
    pl.semaphore_wait(barrier, ngcol + ngrow - 2)

    def span(i):
        return pl.ds(pl.multiple_of(i * chunk, chunk), chunk)

    def send(src, slot, i, sem, target):
        return pltpu.make_async_remote_copy(
            src_ref=src, dst_ref=rows.at[slot, :, span(i), :], send_sem=sem,
            recv_sem=row_sem.at[slot, i], device_id=(r, target), device_id_type=MESH,
        )

    def from_own(i, sems, target):
        return send(e_ref.at[:, span(i), :], c, i, sems.at[q, i], target)

    def from_rows(qt, i, sems, target):
        slot = 2 * qt + k
        return send(rows.at[slot, :, span(i), :], slot, i, sems.at[qt, i], target)

    for i in range(CHUNKS):
        @pl.when(q + 1 < nq)
        def _():
            from_own(i, up_sem, c + 2).start()

        @pl.when(q >= 1)
        def _():
            from_own(i, dn_sem, c - 2).start()

        from_own(i, pt_sem, mate).start()

    def w_copy(qt):
        block = pl.ds(pl.multiple_of(qt * 2 * depth, 2 * depth), 2 * depth)
        return pltpu.make_async_copy(w_ref.at[:, block, :], wbuf, w_sem)

    acc[...] = jnp.zeros_like(acc)

    def spread_copy(src, slot, i, part, target):
        return pltpu.make_async_remote_copy(
            src_ref=src, dst_ref=cols.at[slot, part, span(i), :], send_sem=lay_sem.at[slot, i, part],
            recv_sem=col_sem.at[slot, i, part], device_id=(target, c), device_id_type=MESH,
        )

    def place_copy(qt, b, i):
        return pltpu.make_async_copy(
            rows.at[2 * qt + b, :, span(i), :],
            cols.at[2 * qt + b - k * held, :, span(i), :],
            loc_sem.at[2 * qt + b - k * held, i],
        )

    def mine_half(qt):
        return qt // (nq // 2) == k

    steps = nq * CHUNKS

    def tick(tau, carry):
        @pl.when(tau < steps)
        def _():
            t = tau // CHUNKS
            i = tau % CHUNKS
            qt = order(t)

            @pl.when(i == 0)
            def _():
                w_copy(qt).start()

            @pl.when(tau == 0)
            def _():
                pltpu.make_async_copy(e_ref, rows.at[c], own_sem).wait()

            @pl.when(t > 0)
            def _():
                from_rows(qt, i, pt_sem, mate).wait_recv()

                @pl.when(jnp.logical_and(qt < q, q + 1 < nq))
                def _():
                    from_rows(qt, i, up_sem, c + 2).start()

                @pl.when(jnp.logical_and(qt > q, q >= 1))
                def _():
                    from_rows(qt, i, dn_sem, c - 2).start()

                from_rows(qt, i, pt_sem, mate).start()

            other = 2 * qt + 1 - k
            send(rows.at[other, :, span(i), :], other, i, pt_sem.at[qt, i], mate).wait_recv()

            @pl.when(jnp.logical_and(is_source, mine_half(qt)))
            def _():
                for b in range(2):
                    slot = 2 * qt + b - k * held
                    whole = rows.at[2 * qt + b]
                    spread_copy(whole.at[0, span(i), :], slot, i, 0, after).start()
                    spread_copy(whole.at[1, span(i), :], slot, i, 1, before).start()
                    place_copy(qt, b, i).start()

            @pl.when(i == 0)
            def _():
                w_copy(qt).wait()

            def column(n, carry):
                lanes = pl.ds(pl.multiple_of(n * TILE, TILE), TILE)
                dot = functools.partial(jnp.dot, preferred_element_type=jnp.float32)
                re = acc[0, span(i), lanes]
                im = acc[1, span(i), lanes]
                for b in range(2):
                    mre = rows[2 * qt + b, 0, span(i), :]
                    mim = rows[2 * qt + b, 1, span(i), :]
                    wre = wbuf[0, b * depth:(b + 1) * depth, lanes]
                    wim = wbuf[1, b * depth:(b + 1) * depth, lanes]
                    re += dot(mre, wre) + dot(mim, wim)
                    im += dot(mre, wim) + dot(mim, -wre)
                acc[0, span(i), lanes] = re
                acc[1, span(i), lanes] = im
                return carry

            lax.fori_loop(0, width // TILE, column, 0)

        for part in range(2):
            hops = dist if part == 0 else lax.rem(ngrow - dist, ngrow)
            past = tau - hops

            @pl.when(jnp.logical_and(hops > 0, jnp.logical_and(past >= 0, past < steps)))
            def _():
                t = past // CHUNKS
                i = past % CHUNKS
                qt = order(t)

                @pl.when(mine_half(qt))
                def _():
                    for b in range(2):
                        slot = 2 * qt + b - k * held
                        onward = spread_copy(
                            cols.at[slot, part, span(i), :], slot, i, part,
                            after if part == 0 else before,
                        )
                        onward.wait_recv()

                        @pl.when(hops < ngrow - 1)
                        def _():
                            onward.start()

        return carry

    lax.fori_loop(0, steps + ngrow - 1, tick, 0)

    @pl.when(is_source)
    def _():
        for slot in range(held):
            for i in range(CHUNKS):
                pltpu.make_async_copy(
                    rows.at[k * held + slot, :, span(i), :], cols.at[slot, :, span(i), :],
                    loc_sem.at[slot, i],
                ).wait()

    band = 64

    def contract(p, carry):
        here = pl.ds(pl.multiple_of(p * band, band), band)
        s_re = jnp.zeros((band, 1), jnp.float32)
        s_im = jnp.zeros((band, 1), jnp.float32)
        for slot in range(held):
            lanes = slice(slot * depth, (slot + 1) * depth)
            zre = acc[0, here, lanes]
            zim = acc[1, here, lanes]
            mre = cols[slot, 0, here, :].astype(jnp.float32)
            mim = cols[slot, 1, here, :].astype(jnp.float32)
            s_re += jnp.sum(zre * mre - zim * mim, axis=1, keepdims=True)
            s_im += jnp.sum(zre * mim + zim * mre, axis=1, keepdims=True)
        svec[0, here, :] = s_re
        svec[1, here, :] = s_im
        return carry

    lax.fori_loop(0, pairs // band, contract, 0)

    nb, ne = eidx_ref.shape
    summed = band_ref.shape[1]
    npoint = grid_ref.shape[1]
    energy = grid_ref[...]

    def iota(shape, dim):
        return lax.broadcasted_iota(jnp.int32, shape, dim)

    square = (npoint, npoint)
    energy_col = jnp.sum(jnp.where(iota(square, 0) == iota(square, 1), energy, 0.0), axis=1, keepdims=True)
    diag = (summed, summed)
    index_col = jnp.sum(
        jnp.where(iota(diag, 0) == iota(diag, 1), band_ref[...].astype(jnp.float32), 0.0),
        axis=1, keepdims=True,
    )
    points = iota((summed, npoint), 1).astype(jnp.float32)
    band_energy = jnp.sum(jnp.where(index_col == points, energy, 0.0), axis=1, keepdims=True)
    scale = summed ** (-0.5)
    mine[...] = jnp.zeros_like(mine)
    for n in range(nb):
        chosen = iota((npoint, ne), 0) == eidx_ref[n:n + 1, :]
        eval_energy = jnp.sum(jnp.where(chosen, energy_col, 0.0), axis=0, keepdims=True)
        offset = eval_energy - band_energy
        denom = offset * offset + 0.25
        wre = offset / denom
        wim = -0.5 / denom
        sre = svec[0, n * summed:(n + 1) * summed, :]
        sim = svec[1, n * summed:(n + 1) * summed, :]
        mine[n:n + 1, 0:ne] = scale * jnp.sum(wre * sre - wim * sim, axis=0, keepdims=True)
        mine[nb + n:nb + n + 1, 0:ne] = scale * jnp.sum(wre * sim + wim * sre, axis=0, keepdims=True)

    def exchange(base, count, me, device):
        tiles[base + me] = mine[...]

        def to(step):
            return pltpu.make_async_remote_copy(
                src_ref=mine, dst_ref=tiles.at[base + me], send_sem=t_send.at[base + step],
                recv_sem=t_recv.at[base + me], device_id=device(lax.rem(me + step, count)),
                device_id_type=MESH,
            )

        for step in range(1, count):
            to(step).start()
        for step in range(1, count):
            peer = lax.rem(me + step, count)
            pltpu.make_async_remote_copy(
                src_ref=mine, dst_ref=tiles.at[base + peer], send_sem=t_send.at[base + step],
                recv_sem=t_recv.at[base + peer], device_id=device(peer), device_id_type=MESH,
            ).wait_recv()
        for step in range(1, count):
            to(step).wait_send()
        total = tiles[base]
        for j in range(1, count):
            total += tiles[base + j]
        return total

    mine[...] = exchange(0, ngcol, c, lambda v: (r, v))
    total = exchange(ngcol, ngrow, r, lambda v: (v, c))
    out_ref[0] = total[0:nb, 0:ne]
    out_ref[1] = total[nb:2 * nb, 0:ne]

    def drain(j, carry):
        qt = j // CHUNKS
        i = j % CHUNKS

        @pl.when(jnp.logical_and(qt <= q, q + 1 < nq))
        def _():
            from_rows(qt, i, up_sem, c + 2).wait_send()

        @pl.when(jnp.logical_and(qt >= q, q >= 1))
        def _():
            from_rows(qt, i, dn_sem, c - 2).wait_send()

        from_rows(qt, i, pt_sem, mate).wait_send()
        for part in range(2):
            hops = dist if part == 0 else lax.rem(ngrow - dist, ngrow)

            @pl.when(hops < ngrow - 1)
            def _():
                spread_copy(
                    cols.at[qt, part, span(i), :], qt, i, part, after if part == 0 else before
                ).wait_send()

        return carry

    lax.fori_loop(0, nq * CHUNKS, drain, 0)


def solution(mesh):
    ngrow = mesh.shape["grow"]
    ngcol = mesh.shape["gcol"]
    nq = ngcol // 2

    def local(screened, elements, energy_grid, band_index, energy_index):
        _, pairs, depth = elements.shape
        width = screened.shape[2]
        nb, ne = energy_index.shape
        dma = pltpu.SemaphoreType.DMA
        vmem = pl.BlockSpec(memory_space=pltpu.VMEM)
        hbm = pl.BlockSpec(memory_space=pl.ANY)
        return pl.pallas_call(
            functools.partial(kernel, ngrow, ngcol),
            out_shape=jax.ShapeDtypeStruct((2, nb, ne), jnp.float32),
            in_specs=[hbm, hbm, vmem, vmem, vmem],
            out_specs=vmem,
            scratch_shapes=[
                pltpu.VMEM((ngcol, 2, pairs, depth), jnp.bfloat16),
                pltpu.VMEM((nq, 2, pairs, depth), jnp.bfloat16),
                pltpu.VMEM((2, pairs, width), jnp.float32),
                pltpu.VMEM((2, 2 * depth, width), jnp.bfloat16),
                pltpu.VMEM((2, pairs, 1), jnp.float32),
                pltpu.VMEM((ngcol + ngrow, 2 * nb, 128), jnp.float32),
                pltpu.VMEM((2 * nb, 128), jnp.float32),
                dma((nq, CHUNKS)),
                dma((nq, CHUNKS)),
                dma((nq, CHUNKS)),
                dma((nq, CHUNKS, 2)),
                dma((ngcol, CHUNKS)),
                dma((nq, CHUNKS, 2)),
                dma((nq, CHUNKS)),
                dma,
                dma,
                dma((ngcol + ngrow,)),
                dma((ngcol + ngrow,)),
            ],
            compiler_params=pltpu.CompilerParams(
                collective_id=0, has_side_effects=True, vmem_limit_bytes=60 * 1024 * 1024
            ),
            cost_estimate=pl.CostEstimate(
                flops=8 * pairs * screened.shape[1] * width,
                bytes_accessed=screened.size * 2, transcendentals=0,
            ),
        )(screened, elements, energy_grid[None], band_index[None], energy_index)

    in_specs = (P(None, "grow", "gcol"), P(None, None, ("grow", "gcol")), P(), P(), P())
    return jax.shard_map(local, mesh=mesh, in_specs=in_specs, out_specs=P(), check_vma=False)
```

time: 499 us -> 198 us (0.40)
  waiting for transfers between devices: 325 us -> 0 us
  Pallas kernels: 0 us -> 196 us
  matrix products: 79.4 us -> 0 us
  other arithmetic: 40.1 us -> 0 us
  blocking collectives: 40.1 us -> 0 us
  between operations: 13.5 us -> 0.01 us
    pallas_call x0 -> x1, Pallas kernels: none -> 196 us  [local(): pl.pallas_call(functools.partial(kernel, ngrow, ngcol), out_shape=jax.Sha...]
    psum x1 -> x0, waiting for transfers between devices: 169 us -> none  [spread(): return lax.psum(block, axis)]
    all_gather x1 -> x0, waiting for transfers between devices: 155 us -> none  [local(): row_part = lax.all_gather(elements, 'gcol', axis=2, tiled=True)]
    dot_general x1 -> x0, matrix products: 79.4 us -> none  [local(): jnp.einsum('mph,wgh->mpwg', col_part, screened, preferred_element_type=jn...]
    psum x1 -> x0, blocking collectives: 40.1 us -> none  [local(): total_re, total_im = lax.psum((s_re, s_im), ('grow', 'gcol'))]
    reduce_sum x4 -> x0, other arithmetic: 29.8 us -> none  [the longest x1 28.2 us: local(): s_re = jnp.sum(rre * yre + rim * yim, axis=-1)]
    select_n x1 -> x0, other arithmetic: 9.68 us -> none  [spread(): jnp.where(lax.axis_index(axis) == source, block, jnp.zeros_like(block))]
  transfers between devices with their start and end apart: 2 -> 0, of which waited for: 2 -> 0; matrix products, arithmetic and copies ran while one was open for 0% -> 0% of each run, Pallas kernels for 0% -> 0%
where the time goes in v1:
time: 198 us; the launch traced here: 197 us
  Pallas kernels  196 us (99%)
    pallas_call x1, Pallas kernels, local(): pl.pallas_call(functools.partial(kernel, ngrow, ngcol), out_shape=jax.Sha...  196 us

profile of v1, /device:TPU:0, one launch (start us, length us, event | category | flops | bytes accessed | tf_op | source)
XLA Modules:
  0.0 197.4 jit_solution(14895089653732769975)
XLA Ops:
  0.0 196.2 %shard_map.55 = f32[2,4,16]{2,1,0:T(4,128)} custom-call(bf16[2,4096,2048]{2,1,0:T(8,128)(2,1)} %w_ref.1, bf16[2,1024,512]{2,1,0:T(8,128)(2,1)} %e_ref.1, f32[1,256]{1,0:T(1,128)} %bitcast.2, s32[1,256]{1,0:T(1,128)} %bitcast.3, s32[4,16]{1,0:T(4,128)} %eidx_ref.1), custom_call_target="tpu_custom_call" | custom-call | flops 68719476736 | bytes 33554432 | tf_op jit(solution)/shard_map/pallas_call | solution.py:334
  196.2 1.3 copy.7

commit v2 on v1

--- a/solution.py
+++ b/solution.py
@@ -8,7 +8,7 @@
 from jax.sharding import PartitionSpec as P
 
 MESH = pl.DeviceIdType.MESH
-CHUNKS = 4
+CHUNKS = 8
 TILE = 512
 
 
@@ -42,7 +42,8 @@
     near = jnp.minimum(q, nq - 1 - q)
 
     def order(t):
-        alternate = jnp.where(t % 2 == 1, q - (t + 1) // 2, q + t // 2)
+        ahead = jnp.where(q > near, -1, 1)
+        alternate = jnp.where(t % 2 == 1, q + ahead * ((t + 1) // 2), q - ahead * (t // 2))
         rest = jnp.where(q > near, q - (t - near), q + (t - near))
         return jnp.where(t <= 2 * near, alternate, rest)
 
@@ -110,106 +111,6 @@
         return qt // (nq // 2) == k
 
     steps = nq * CHUNKS
-
-    def tick(tau, carry):
-        @pl.when(tau < steps)
-        def _():
-            t = tau // CHUNKS
-            i = tau % CHUNKS
-            qt = order(t)
-
-            @pl.when(i == 0)
-            def _():
-                w_copy(qt).start()
-
-            @pl.when(tau == 0)
-            def _():
-                pltpu.make_async_copy(e_ref, rows.at[c], own_sem).wait()
-
-            @pl.when(t > 0)
-            def _():
-                from_rows(qt, i, pt_sem, mate).wait_recv()
-
-                @pl.when(jnp.logical_and(qt < q, q + 1 < nq))
-                def _():
-                    from_rows(qt, i, up_sem, c + 2).start()
-
-                @pl.when(jnp.logical_and(qt > q, q >= 1))
-                def _():
-                    from_rows(qt, i, dn_sem, c - 2).start()
-
-                from_rows(qt, i, pt_sem, mate).start()
-
-            other = 2 * qt + 1 - k
-            send(rows.at[other, :, span(i), :], other, i, pt_sem.at[qt, i], mate).wait_recv()
-
-            @pl.when(jnp.logical_and(is_source, mine_half(qt)))
-            def _():
-                for b in range(2):
-                    slot = 2 * qt + b - k * held
-                    whole = rows.at[2 * qt + b]
-                    spread_copy(whole.at[0, span(i), :], slot, i, 0, after).start()
-                    spread_copy(whole.at[1, span(i), :], slot, i, 1, before).start()
-                    place_copy(qt, b, i).start()
-
-            @pl.when(i == 0)
-            def _():
-                w_copy(qt).wait()
-
-            def column(n, carry):
-                lanes = pl.ds(pl.multiple_of(n * TILE, TILE), TILE)
-                dot = functools.partial(jnp.dot, preferred_element_type=jnp.float32)
-                re = acc[0, span(i), lanes]
-                im = acc[1, span(i), lanes]
-                for b in range(2):
-                    mre = rows[2 * qt + b, 0, span(i), :]
-                    mim = rows[2 * qt + b, 1, span(i), :]
-                    wre = wbuf[0, b * depth:(b + 1) * depth, lanes]
-                    wim = wbuf[1, b * depth:(b + 1) * depth, lanes]
-                    re += dot(mre, wre) + dot(mim, wim)
-                    im += dot(mre, wim) + dot(mim, -wre)
-                acc[0, span(i), lanes] = re
-                acc[1, span(i), lanes] = im
-                return carry
-
-            lax.fori_loop(0, width // TILE, column, 0)
-
-        for part in range(2):
-            hops = dist if part == 0 else lax.rem(ngrow - dist, ngrow)
-            past = tau - hops
-
-            @pl.when(jnp.logical_and(hops > 0, jnp.logical_and(past >= 0, past < steps)))
-            def _():
-                t = past // CHUNKS
-                i = past % CHUNKS
-                qt = order(t)
-
-                @pl.when(mine_half(qt))
-                def _():
-                    for b in range(2):
-                        slot = 2 * qt + b - k * held
-                        onward = spread_copy(
-                            cols.at[slot, part, span(i), :], slot, i, part,
-                            after if part == 0 else before,
-                        )
-                        onward.wait_recv()
-
-                        @pl.when(hops < ngrow - 1)
-                        def _():
-                            onward.start()
-
-        return carry
-
-    lax.fori_loop(0, steps + ngrow - 1, tick, 0)
-
-    @pl.when(is_source)
-    def _():
-        for slot in range(held):
-            for i in range(CHUNKS):
-                pltpu.make_async_copy(
-                    rows.at[k * held + slot, :, span(i), :], cols.at[slot, :, span(i), :],
-                    loc_sem.at[slot, i],
-                ).wait()
 
     band = 64
 
@@ -229,7 +130,133 @@
         svec[1, here, :] = s_im
         return carry
 
-    lax.fori_loop(0, pairs // band, contract, 0)
+    def tick(tau, carry):
+        @pl.when(tau < steps)
+        def _():
+            t = tau // CHUNKS
+            i = tau % CHUNKS
+            qt = order(t)
+
+            @pl.when(i == 0)
+            def _():
+                w_copy(qt).start()
+
+            @pl.when(tau == 0)
+            def _():
+                pltpu.make_async_copy(e_ref, rows.at[c], own_sem).wait()
+
+            @pl.when(t > 0)
+            def _():
+                from_rows(qt, i, pt_sem, mate).wait_recv()
+
+                @pl.when(jnp.logical_and(qt < q, q + 1 < nq))
+                def _():
+                    from_rows(qt, i, up_sem, c + 2).start()
+
+                @pl.when(jnp.logical_and(qt > q, q >= 1))
+                def _():
+                    from_rows(qt, i, dn_sem, c - 2).start()
+
+                from_rows(qt, i, pt_sem, mate).start()
+
+            other = 2 * qt + 1 - k
+            send(rows.at[other, :, span(i), :], other, i, pt_sem.at[qt, i], mate).wait_recv()
+
+            @pl.when(jnp.logical_and(is_source, mine_half(qt)))
+            def _():
+                for b in range(2):
+                    slot = 2 * qt + b - k * held
+                    whole = rows.at[2 * qt + b]
+                    spread_copy(whole.at[0, span(i), :], slot, i, 0, after).start()
+                    spread_copy(whole.at[1, span(i), :], slot, i, 1, before).start()
+                    place_copy(qt, b, i).start()
+
+        for part in range(2):
+            hops = dist if part == 0 else lax.rem(ngrow - dist, ngrow)
+            past = tau - hops
+
+            @pl.when(jnp.logical_and(hops > 0, jnp.logical_and(past >= 0, past < steps)))
+            def _():
+                t = past // CHUNKS
+                i = past % CHUNKS
+                qt = order(t)
+
+                @pl.when(mine_half(qt))
+                def _():
+                    for b in range(2):
+                        slot = 2 * qt + b - k * held
+                        onward = spread_copy(
+                            cols.at[slot, part, span(i), :], slot, i, part,
+                            after if part == 0 else before,
+                        )
+                        onward.wait_recv()
+
+                        @pl.when(hops < ngrow - 1)
+                        def _():
+                            onward.start()
+
+        @pl.when(tau < steps)
+        def _():
+            t = tau // CHUNKS
+            i = tau % CHUNKS
+            qt = order(t)
+
+            def multiply(first, size):
+                here = pl.ds(pl.multiple_of(first, size), size)
+
+                def column(n, carry):
+                    lanes = pl.ds(pl.multiple_of(n * TILE, TILE), TILE)
+                    dot = functools.partial(jnp.dot, preferred_element_type=jnp.float32)
+                    re = acc[0, here, lanes]
+                    im = acc[1, here, lanes]
+                    for b in range(2):
+                        mre = rows[2 * qt + b, 0, here, :]
+                        mim = rows[2 * qt + b, 1, here, :]
+                        wre = wbuf[0, b * depth:(b + 1) * depth, lanes]
+                        wim = wbuf[1, b * depth:(b + 1) * depth, lanes]
+                        re += dot(mre, wre) + dot(mim, wim)
+                        im += dot(mre, wim) + dot(mim, -wre)
+                    acc[0, here, lanes] = re
+                    acc[1, here, lanes] = im
+                    return carry
+
+                lax.fori_loop(0, width // TILE, column, 0)
+
+            @pl.when(i == 1)
+            def _():
+                @pl.when(t < nq - 1)
+                def _():
+                    w_copy(qt).wait()
+
+            @pl.when(jnp.logical_and(i == 0, t == nq - 1))
+            def _():
+                w_copy(qt).wait()
+
+            @pl.when(jnp.logical_and(i % 2 == 1, t < nq - 1))
+            def _():
+                multiply((i - 1) * chunk, 2 * chunk)
+
+            @pl.when(t == nq - 1)
+            def _():
+                multiply(i * chunk, chunk)
+
+        done = tau - (steps - CHUNKS) - (ngrow - 1)
+
+        @pl.when(done >= 0)
+        def _():
+            @pl.when(is_source)
+            def _():
+                for slot in range(held):
+                    pltpu.make_async_copy(
+                        rows.at[k * held + slot, :, span(done), :], cols.at[slot, :, span(done), :],
+                        loc_sem.at[slot, done],
+                    ).wait()
+
+            lax.fori_loop(done * (chunk // band), (done + 1) * (chunk // band), contract, 0)
+
+        return carry
+
+    lax.fori_loop(0, steps + ngrow - 1, tick, 0)
 
     nb, ne = eidx_ref.shape
     summed = band_ref.shape[1]

time: 198 us -> 206 us (1.040)
  Pallas kernels: 196 us -> 205 us
    pallas_call x1, Pallas kernels: 196 us -> 205 us  [local(): pl.pallas_call(functools.partial(kernel, ngrow, ngcol), out_shape=jax.Sha...]
where the time goes in v2:
time: 206 us
  Pallas kernels  205 us (100%)
    pallas_call x1, Pallas kernels, local(): pl.pallas_call(functools.partial(kernel, ngrow, ngcol), out_shape=jax.Sha...  205 us

profile of v2, /device:TPU:0, one launch (start us, length us, event | category | flops | bytes accessed | tf_op | source)
XLA Modules:
  0.0 206.1 jit_solution(13695253315928376575)
XLA Ops:
  0.0 204.8 %shard_map.55 = f32[2,4,16]{2,1,0:T(4,128)} custom-call(bf16[2,4096,2048]{2,1,0:T(8,128)(2,1)} %w_ref.1, bf16[2,1024,512]{2,1,0:T(8,128)(2,1)} %e_ref.1, f32[1,256]{1,0:T(1,128)} %bitcast.2, s32[1,256]{1,0:T(1,128)} %bitcast.3, s32[4,16]{1,0:T(4,128)} %eidx_ref.1), custom_call_target="tpu_custom_call" | custom-call | flops 68719476736 | bytes 33554432 | tf_op jit(solution)/shard_map/pallas_call | solution.py:361
  204.8 1.3 copy.7
